TPU v7x, 32 devices: a whole 2x2x4 slice. The times are simulated.
32 devices in a mesh: gx: 8 (over y, x, core), gy: 4 (over z).
Axes of the slice: x: 2, y: 2, z: 4, core: 2. Of those that a mesh axis runs over, the one named last changes fastest.
Arguments:
- control: float32 [6, 2048, 1024], P(None, 'gy', 'gx'), may hold values from -6 to 6
- field_scale: float32 [6], replicated, may hold values from 0.5 to 2
- water_depth: float32 [2048, 1024], P('gy', 'gx'), may hold values from 0.5 to 4
- bed_mobility: float32 [2048, 1024], P('gy', 'gx'), may hold values from 0.1 to 1
- footprint: int32 [32, 32, 8], P(('gx', 'gy')), may hold values from 0 to 511
- instrument: int32 [32, 32, 8], P(('gx', 'gy')), may hold values from 0 to 1
- live_counts: int32 [32, 32], P(('gx', 'gy')), may hold values from 0 to 8, as said below
- observed: float32 [32, 32, 8, 128], P(('gx', 'gy')), may hold values from -6 to 6
- obs_precision: float32 [2, 128, 128], replicated, may hold values from -0.001 to 0.012, as said below
Outputs:
- gradient: float32 [6, 2048, 1024], P(None, 'gy', 'gx')
Inputs may be any that keep to these rules, and one draw needn't show every extreme that they name: `live_counts`: every owner has at least one source device whose 8 slots are all live. `obs_precision`: Symmetric; every diagonal entry exceeds the sum of the magnitudes of the other entries of its row.
All inputs are finite; a program needn't handle non-finite values.
Results may differ from a plain program's by a relative error of at most 0.0001.
Values sent between devices are 32-bit elements; how exact they have to be, the bound alone decides.
A program may use at most 64 MiB of HBM per device.

v0:
```python
import functools

import jax
import jax.numpy as jnp
from jax import lax
from jax.experimental import pallas as pl
from jax.experimental.pallas import tpu as pltpu
from jax.sharding import PartitionSpec as P

HALF = 128
BLK = 128
STEPS = 3


TIME_STEP = 0.2
GRAVITY = 1.0
FRICTION = 0.5
DIFFUSION = (0.4, 0.25)
SETTLING = (0.5, 0.2)


def with_halo(block, sides, width):
    for axis, dim in sides:
        count = lax.axis_size(axis)
        forward = [(i, i + 1) for i in range(count - 1)]
        backward = [(target, source) for source, target in forward]
        low = lax.ppermute(
            lax.slice_in_dim(block, block.shape[dim] - width, None, axis=dim), axis, forward
        )
        high = lax.ppermute(lax.slice_in_dim(block, 0, width, axis=dim), axis, backward)
        block = jnp.concatenate([low, block, high], axis=dim)
    return block


def band_table():
    window = jnp.arange(3 * HALF, dtype=jnp.int32)[:, None]
    column = jnp.arange(HALF, dtype=jnp.int32)[None, :]
    offsets = (window - column - HALF).astype(jnp.float32)
    corr_length = HALF / 2.0
    inside = jnp.abs(offsets) <= HALF
    kernel = jnp.where(inside, jnp.exp(-offsets * offsets / (2.0 * corr_length * corr_length)), 0.0)
    tap_offsets = jnp.arange(-HALF, HALF + 1, dtype=jnp.int32).astype(jnp.float32)
    norm_sum = jnp.sqrt(jnp.sum(jnp.exp(-tap_offsets * tap_offsets / (corr_length * corr_length))))
    return kernel / norm_sum


def split(value):
    high = value.astype(jnp.bfloat16)
    return high, (value - high.astype(jnp.float32)).astype(jnp.bfloat16)


def mul(left, right):
    return jnp.dot(left, right, preferred_element_type=jnp.float32)


def mul_pair(left, right):
    return mul(left[0], right[0]) + mul(left[0], right[1]) + mul(left[1], right[0])


def neighbours(names, counts):
    found = []
    for axis, count in zip(names, counts):
        me = lax.axis_index(axis)
        found.append((axis, me - 1, me > 0))
        found.append((axis, me + 1, me < count - 1))
    return found


def greet(around):
    barrier = pltpu.get_barrier_semaphore()
    for axis, other, there in around:

        @pl.when(there)
        def _():
            pl.semaphore_signal(
                barrier, inc=1, device_id={axis: other}, device_id_type=pl.DeviceIdType.MESH
            )

    pl.semaphore_wait(barrier, sum(there.astype(jnp.int32) for _, _, there in around))


def correlate_kernel(
    counts, x_ref, taps_ref, out_ref, low_x, high_x, low_y, high_y, wide, high_ref, low_ref, send, recv
):
    fields, rows, cols = x_ref.shape
    around = neighbours(("gx", "gy"), counts)
    greet(around)

    def taps(index):
        part = pl.ds(index * HALF, HALF)
        return high_ref[part, :], low_ref[part, :]

    def copy(field, side):
        axis, other, _ = around[side]
        if side == 0:
            source, target = x_ref.at[field], high_x.at[field]
        elif side == 1:
            source, target = x_ref.at[field], low_x.at[field]
        elif side == 2:
            source, target = wide.at[field, pl.ds(0, HALF)], high_y.at[field]
        else:
            source, target = wide.at[field, pl.ds(rows - HALF, HALF)], low_y.at[field]
        return pltpu.make_async_remote_copy(
            src_ref=source,
            dst_ref=target,
            send_sem=send.at[side, field],
            recv_sem=recv.at[side, field],
            device_id={axis: other},
            device_id_type=pl.DeviceIdType.MESH,
        )

    def start_x(field, carry):
        for side in (0, 1):

            @pl.when(around[side][2])
            def _():
                copy(field, side).start()

        return carry

    lax.fori_loop(0, fields, start_x, 0)
    for there, halo in (
        (around[0][2], low_x),
        (around[1][2], high_x),
        (around[2][2], low_y),
        (around[3][2], high_y),
    ):

        @pl.when(jnp.logical_not(there))
        def _():
            halo[...] = jnp.zeros_like(halo)

    high_ref[...], low_ref[...] = split(taps_ref[...])

    def own(field, carry):
        wide[field] = mul_pair(split(x_ref[field]), taps(1))
        return carry

    lax.fori_loop(0, fields, own, 0)

    def columns(field, carry):
        @pl.when(around[0][2])
        def _():
            copy(field, 1).wait_recv()

        @pl.when(around[1][2])
        def _():
            copy(field, 0).wait_recv()

        wide[field] = (
            wide[field]
            + mul_pair(split(low_x[field]), taps(0))
            + mul_pair(split(high_x[field]), taps(2))
        )
        for side in (2, 3):

            @pl.when(around[side][2])
            def _():
                copy(field, side).start()

        pieces = [split(wide[field, pl.ds(t * HALF, HALF), :]) for t in range(rows // HALF)]
        for t, piece in enumerate(pieces):
            total = mul_pair(taps(1), piece)
            if t > 0:
                total = total + mul_pair(taps(2), pieces[t - 1])
            if t < len(pieces) - 1:
                total = total + mul_pair(taps(0), pieces[t + 1])
            out_ref[field, pl.ds(t * HALF, HALF), :] = total
        return carry

    lax.fori_loop(0, fields, columns, 0)

    def edges(field, carry):
        @pl.when(around[2][2])
        def _():
            copy(field, 3).wait_recv()

        @pl.when(around[3][2])
        def _():
            copy(field, 2).wait_recv()

        first, last = pl.ds(0, HALF), pl.ds(rows - HALF, HALF)
        out_ref[field, first, :] = out_ref[field, first, :] + mul_pair(taps(2), split(low_y[field]))
        out_ref[field, last, :] = out_ref[field, last, :] + mul_pair(taps(0), split(high_y[field]))
        for side in range(4):

            @pl.when(around[side][2])
            def _():
                copy(field, side).wait_send()

        return carry

    lax.fori_loop(0, fields, edges, 0)


def correlate(block, kernel, name):
    fields, rows, cols = block.shape
    counts = (lax.axis_size("gx"), lax.axis_size("gy"))
    full = pl.BlockSpec(memory_space=pltpu.VMEM)
    edge = pltpu.VMEM((fields, HALF, cols), jnp.float32)
    side = pltpu.VMEM((fields, rows, cols), jnp.float32)
    return pl.pallas_call(
        functools.partial(correlate_kernel, counts),
        out_shape=jax.ShapeDtypeStruct(block.shape, jnp.float32),
        in_specs=[full] * 2,
        out_specs=full,
        scratch_shapes=[
            side,
            side,
            edge,
            edge,
            side,
            pltpu.VMEM(kernel.shape, jnp.bfloat16),
            pltpu.VMEM(kernel.shape, jnp.bfloat16),
            pltpu.SemaphoreType.DMA((4, fields)),
            pltpu.SemaphoreType.DMA((4, fields)),
        ],
        compiler_params=pltpu.CompilerParams(
            collective_id=name, has_side_effects=True, vmem_limit_bytes=40 * 2**20
        ),
        cost_estimate=pl.CostEstimate(
            flops=36 * fields * rows * cols * HALF,
            bytes_accessed=8 * fields * rows * cols,
            transcendentals=0,
        ),
    )(block, kernel)


def observation_sums(rows, footprint, instrument, live_counts, observed):
    slots = footprint.shape[1]
    live = jnp.arange(slots, dtype=jnp.int32)[None, :] < live_counts[:, None]
    code = jnp.where(live, instrument + 1, 0).astype(jnp.float32)
    code = jnp.pad(code, ((0, 0), (0, BLK - slots)))[:, None, :]
    sent = jnp.concatenate([observed, code], axis=1)
    came = lax.all_to_all(sent, ("gx", "gy"), split_axis=0, concat_axis=0, tiled=True)
    values = came[:, :slots].reshape(-1, BLK)
    kinds = came[:, slots, :slots].reshape(-1)
    here = footprint.reshape(-1)[None, :] == jnp.arange(rows, dtype=jnp.int32)[:, None]
    sums = []
    for kind in (1.0, 2.0):
        picked = (here & (kinds == kind)[None, :]).astype(jnp.float32)
        sums.append(
            (
                jnp.sum(picked, axis=1, keepdims=True),
                jnp.dot(picked, values, precision=lax.Precision.HIGHEST),
            )
        )
    return sums


def slope_x(padded):
    return 0.5 * (padded[:, 1:-1, 2:] - padded[:, 1:-1, :-2])


def slope_y(padded):
    return 0.5 * (padded[:, 2:, 1:-1] - padded[:, :-2, 1:-1])


def laplace(padded):
    return (
        padded[:, 2:, 1:-1]
        + padded[:, :-2, 1:-1]
        + padded[:, 1:-1, 2:]
        + padded[:, 1:-1, :-2]
        - 4.0 * padded[:, 1:-1, 1:-1]
    )


def inside_grid(margin, rows, cols):
    row_ids = lax.axis_index("gy") * rows + jnp.arange(rows + 2 * margin, dtype=jnp.int32) - margin
    col_ids = lax.axis_index("gx") * cols + jnp.arange(cols + 2 * margin, dtype=jnp.int32) - margin
    row_ok = (row_ids >= 0) & (row_ids < rows * lax.axis_size("gy"))
    col_ok = (col_ids >= 0) & (col_ids < cols * lax.axis_size("gx"))
    return (row_ok[:, None] & col_ok[None, :]).astype(jnp.float32)


def trim(plane):
    return plane[1:-1, 1:-1]


def trim_two(plane):
    return plane[2:-2, 2:-2]


def region_step(fields, depth, mobility, inside):
    height, speed_x, speed_y, bed_level, silt_one, silt_two = (
        fields[0],
        fields[1],
        fields[2],
        fields[3],
        fields[4],
        fields[5],
    )
    fluxes = jnp.stack(
        [
            depth * speed_x,
            depth * speed_y,
            mobility * speed_x,
            mobility * speed_y,
            silt_one,
            silt_two,
        ]
    )
    along_x = slope_x(fluxes[:4])
    along_y = slope_y(fluxes[:4])
    spread = laplace(fluxes[4:])
    middle = trim(inside)
    height_new = (trim(height) - TIME_STEP * (along_x[0] + along_y[1])) * middle
    bed_new = (
        trim(bed_level)
        - TIME_STEP * (along_x[2] + along_y[3])
        + TIME_STEP * (SETTLING[0] * trim(silt_one) + SETTLING[1] * trim(silt_two))
    ) * middle
    silt_one_new = (
        trim(silt_one)
        + TIME_STEP * DIFFUSION[0] * spread[0]
        - TIME_STEP * SETTLING[0] * trim(silt_one)
    ) * middle
    silt_two_new = (
        trim(silt_two)
        + TIME_STEP * DIFFUSION[1] * spread[1]
        - TIME_STEP * SETTLING[1] * trim(silt_two)
    ) * middle
    surface = (height_new + bed_new)[None]
    core = trim_two(inside)
    speed_x_new = (
        (1.0 - TIME_STEP * FRICTION) * trim_two(speed_x) - TIME_STEP * GRAVITY * slope_x(surface)[0]
    ) * core
    speed_y_new = (
        (1.0 - TIME_STEP * FRICTION) * trim_two(speed_y) - TIME_STEP * GRAVITY * slope_y(surface)[0]
    ) * core
    return jnp.stack(
        [
            trim(height_new),
            speed_x_new,
            speed_y_new,
            trim(bed_new),
            trim(silt_one_new),
            trim(silt_two_new),
        ]
    )


def region_adjoint(adjoint, depth, mobility, inside):
    adj_height, adj_speed_x, adj_speed_y, adj_bed, adj_silt_one, adj_silt_two = (
        adjoint[0],
        adjoint[1],
        adjoint[2],
        adjoint[3],
        adjoint[4],
        adjoint[5],
    )
    adj_surface = (
        TIME_STEP * GRAVITY * (slope_x(adj_speed_x[None])[0] + slope_y(adj_speed_y[None])[0])
    )
    middle = trim(inside)
    height_mid = (trim(adj_height) + adj_surface) * middle
    bed_mid = (trim(adj_bed) + adj_surface) * middle
    levels = jnp.stack([height_mid, bed_mid, trim(adj_silt_one), trim(adj_silt_two)])
    grad_x = TIME_STEP * slope_x(levels[:2])
    grad_y = TIME_STEP * slope_y(levels[:2])
    spread = laplace(levels[2:])
    core = trim_two(inside)
    bed_core = trim(bed_mid)
    new_speed_x = (
        (1.0 - TIME_STEP * FRICTION) * trim_two(adj_speed_x)
        + trim_two(depth) * grad_x[0]
        + trim_two(mobility) * grad_x[1]
    ) * core
    new_speed_y = (
        (1.0 - TIME_STEP * FRICTION) * trim_two(adj_speed_y)
        + trim_two(depth) * grad_y[0]
        + trim_two(mobility) * grad_y[1]
    ) * core
    new_silt_one = (
        trim_two(adj_silt_one)
        + TIME_STEP * DIFFUSION[0] * spread[0]
        - TIME_STEP * SETTLING[0] * trim_two(adj_silt_one)
        + TIME_STEP * SETTLING[0] * bed_core
    ) * core
    new_silt_two = (
        trim_two(adj_silt_two)
        + TIME_STEP * DIFFUSION[1] * spread[1]
        - TIME_STEP * SETTLING[1] * trim_two(adj_silt_two)
        + TIME_STEP * SETTLING[1] * bed_core
    ) * core
    return jnp.stack(
        [trim(height_mid), new_speed_x, new_speed_y, bed_core, new_silt_one, new_silt_two]
    )


def on_device(
    control,
    field_scale,
    water_depth,
    bed_mobility,
    footprint,
    instrument,
    live_counts,
    observed,
    obs_precision,
):
    kernel = band_table()
    scales = field_scale[:, None, None]
    rows = water_depth.shape[0]
    cols = water_depth.shape[1]
    (count_sar, sum_sar), (count_lidar, sum_lidar) = observation_sums(
        rows, footprint[0], instrument[0], live_counts[0], observed[0]
    )
    fields = scales * correlate(control, kernel, 1)
    margin = 2 * STEPS
    stacked = jnp.concatenate([fields, water_depth[None], bed_mobility[None]])
    extended = with_halo(stacked, (("gx", 2), ("gy", 1)), margin)
    depth_wide = extended[6]
    mobility_wide = extended[7]
    inside_wide = inside_grid(margin, rows, cols)
    fields = extended[:6]
    depth_now, mobility_now, inside_now = (depth_wide, mobility_wide, inside_wide)
    for _ in range(STEPS):
        fields = region_step(fields, depth_now, mobility_now, inside_now)
        depth_now, mobility_now, inside_now = (
            trim_two(depth_now),
            trim_two(mobility_now),
            trim_two(inside_now),
        )
    misfit_sar = count_sar * (fields[0] + fields[3]) - sum_sar
    misfit_lidar = count_lidar * fields[3] - sum_lidar
    weighted_sar = jnp.einsum(
        "rj,ij->ri", misfit_sar, obs_precision[0], precision=lax.Precision.HIGHEST
    )
    weighted_lidar = jnp.einsum(
        "rj,ij->ri", misfit_lidar, obs_precision[1], precision=lax.Precision.HIGHEST
    )
    planes = jnp.stack([weighted_sar, weighted_sar + weighted_lidar])
    wide_planes = with_halo(planes, (("gx", 2), ("gy", 1)), margin)
    empty_plane = jnp.zeros_like(wide_planes[0])
    adjoint = jnp.stack(
        [wide_planes[0], empty_plane, empty_plane, wide_planes[1], empty_plane, empty_plane]
    )
    depth_now, mobility_now, inside_now = (depth_wide, mobility_wide, inside_wide)
    for _ in range(STEPS):
        adjoint = region_adjoint(adjoint, depth_now, mobility_now, inside_now)
        depth_now, mobility_now, inside_now = (
            trim_two(depth_now),
            trim_two(mobility_now),
            trim_two(inside_now),
        )
    return control + correlate(scales * adjoint, kernel, 2)


def solution(mesh):
    in_specs = (
        P(None, "gy", "gx"),
        P(),
        P("gy", "gx"),
        P("gy", "gx"),
        P(("gx", "gy"), None, None),
        P(("gx", "gy"), None, None),
        P(("gx", "gy"), None),
        P(("gx", "gy"), None, None, None),
        P(),
    )
    out_specs = P(None, "gy", "gx")
    return jax.shard_map(
        on_device, mesh=mesh, in_specs=in_specs, out_specs=out_specs, check_vma=False
    )
```

profile of v0, /device:TPU:4, one launch (start us, length us, event | category | flops | bytes accessed | tf_op | source)
XLA Modules:
  0.0 195.2 jit_solution(13538939361076249344)
XLA Ops:
  1.4 1.4 copy-done
  2.8 41.9 %shard_map.91 = f32[6,512,128]{2,1,0:T(8,128)S(1)} custom-call(f32[6,512,128]{2,1,0:T(8,128)S(1)} %copy-done, f32[384,128]{1,0:T(8,128)S(1)} %fusion.193.taps_ref), custom_call_target="tpu_custom_call" | custom-call | flops 1811939328 | bytes 3145728 | tf_op jit(solution)/shard_map/pallas_call | solution.py:202
  46.0 2.6 %fusion.216 = (f32[8,512,6]{2,1,0:T(8,128)}, f32[8,512,6]{2,1,0:T(8,128)}) fusion(f32[8,512,128]{2,1,0:T(8,128)S(1)} %pad_maximum_fusion.4), kind=kLoop, calls=%fused_computation.387 | loop fusion | bytes 393216 | tf_op jit(solution)/shard_map/slice | solution.py:28
  48.6 2.2 %copy.31 = f32[8,512,6]{1,0,2:T(8,128)S(1)} copy(f32[8,512,6]{2,1,0:T(8,128)} %get-tuple-element.52) | data formatting | bytes 196608 | tf_op jit(solution)/shard_map/slice | solution.py:30
  50.9 2.7 %collective-permute-start.1 = (f32[8,512,6]{1,0,2:T(8,128)S(1)}, f32[8,512,6]{1,0,2:T(8,128)S(1)}, u32[]{:S(2)}, u32[]{:S(2)}) collective-permute-start(f32[8,512,6]{1,0,2:T(8,128)S(1)} %copy.31), channel_id=1, source_target_pairs={{4,0},{8,4},{12,8},{16,12},{20,16},{24,20},{28,24},{5,1},{9,5},{13... | collective-permute-start | bytes 294920 | tf_op jit(solution)/shard_map/ppermute | solution.py:30
  53.6 2.2 %copy.30 = f32[8,512,6]{1,0,2:T(8,128)S(1)} copy(f32[8,512,6]{2,1,0:T(8,128)} %get-tuple-element.51) | data formatting | bytes 196608 | tf_op jit(solution)/shard_map/slice | solution.py:28
  55.8 1.9 collective-permute-start
  58.6 5.3 %all-to-all-start = ((f32[32,9,128]{2,1,0:T(8,128)}), f32[32,9,128]{2,1,0:T(8,128)}, u32[]{:S(2)}, u32[]{:S(2)}) async-start(f32[32,9,128]{2,1,0:T(8,128)} %pad_maximum_fusion.13), calls=%async_computation | async-start | bytes 524288 | tf_op jit(solution)/shard_map/all_to_all | solution.py:235
  64.0 2.0 %copy.33 = f32[8,512,6]{2,1,0:T(8,128)} copy(f32[8,512,6]{1,0,2:T(8,128)S(1)} %collective-permute-done.1) | data formatting | bytes 196608 | tf_op jit(solution)/shard_map/ppermute | solution.py:30
  66.0 2.0 %copy.32 = f32[8,512,6]{2,1,0:T(8,128)} copy(f32[8,512,6]{1,0,2:T(8,128)S(1)} %collective-permute-done) | data formatting | bytes 196608 | tf_op jit(solution)/shard_map/ppermute | solution.py:27
  69.0 1.3 collective-permute-start.3
  70.3 4.5 %collective-permute-start.2 = (f32[8,6,140]{2,1,0:T(8,128)S(1)}, f32[8,6,140]{2,1,0:T(8,128)S(1)}, u32[]{:S(2)}, u32[]{:S(2)}) collective-permute-start(f32[8,6,140]{2,1,0:T(8,128)S(1)} %get-tuple-element.27), channel_id=1, source_target_pairs={{0,1},{1,2},{2,3},{4,5},{5,6},{6,7},{8,9},{9,10},{10,11},{12,13},{... | collective-permute-start | bytes 80648 | tf_op jit(solution)/shard_map/ppermute | solution.py:27
  76.7 5.6 %pad_maximum_fusion = f32[8,524,140]{2,1,0:T(8,128)S(1)} fusion(f32[8,6,140]{2,1,0:T(8,128)S(1)} %collective-permute-done.3, f32[8,512,6]{2,1,0:T(8,128)} %copy.33, f32[1,512,128]{2,1,0:T(8,128)S(1)} %bitcast.361, f32[1,512,128]{2,1,0:T(8,128)S(1)} %bitcast.364, f32[6,512,128]{2,1,0:T(8,128)S(1)} %broadcast_multiply_fusion.1, f32[8,512,6]{2,1,0:T(8,128)} %copy.32, ...), kind=kLoop, calls=%fused_computation | loop fusion | flops 3521280 | bytes 4695040 | tf_op jit(solution)/shard_map/concatenate | solution.py:31
  82.9 1.2 fusion.7
  84.3 1.8 fusion.1
  86.9 1.0 multiply_bitcast_fusion.7
  88.4 1.7 fusion.5
  91.3 1.1 multiply_bitcast_fusion.3
  92.8 1.7 fusion.3
  94.5 14.3 %fusion.32 = f32[2,518,134]{2,1,0:T(8,128)S(1)} fusion(f32[1,520,136]{2,1,0:T(8,128)S(1)} %get-tuple-element.93, f32[1,520,136]{2,1,0:T(8,128)S(1)} %get-tuple-element.92), kind=kLoop, calls=%fused_computation.93 | loop fusion | flops 1388240 | bytes 1121056 | tf_op jit(solution)/shard_map/sub | solution.py:261
  113.0 1.6 convolution_subtract_fusion.1
  114.9 1.3 convolution_subtract_fusion
  116.8 2.0 %collective-permute-start.5 = (f32[2,512,6]{2,1,0:T(8,128)S(1)}, f32[2,512,6]{2,1,0:T(8,128)S(1)}, u32[]{:S(2)}, u32[]{:S(2)}) collective-permute-start(f32[2,512,6]{2,1,0:T(8,128)S(1)} %get-tuple-element.91), channel_id=1, source_target_pairs={{4,0},{8,4},{12,8},{16,12},{20,16},{24,20},{28,24},{5,1},{9,5},{13... | collective-permute-start | bytes 73736 | tf_op jit(solution)/shard_map/ppermute | solution.py:30
  118.9 2.3 %collective-permute-start.4 = (f32[2,512,6]{2,1,0:T(8,128)S(1)}, f32[2,512,6]{2,1,0:T(8,128)S(1)}, u32[]{:S(2)}, u32[]{:S(2)}) collective-permute-start(f32[2,512,6]{2,1,0:T(8,128)S(1)} %get-tuple-element.90), channel_id=1, source_target_pairs={{0,4},{4,8},{8,12},{12,16},{16,20},{20,24},{24,28},{1,5},{5,9},{9,... | collective-permute-start | bytes 73736 | tf_op jit(solution)/shard_map/ppermute | solution.py:27
  121.2 7.2 %collective-permute-done.5 = f32[2,512,6]{2,1,0:T(8,128)S(1)} collective-permute-done((f32[2,512,6]{2,1,0:T(8,128)S(1)}, f32[2,512,6]{2,1,0:T(8,128)S(1)}, u32[]{:S(2)}, u32[]{:S(2)}) %collective-permute-start.5) | collective-permute-done | bytes 24608 | tf_op jit(solution)/shard_map/ppermute | solution.py:30
  128.4 4.6 %collective-permute-done.4 = f32[2,512,6]{2,1,0:T(8,128)S(1)} collective-permute-done((f32[2,512,6]{2,1,0:T(8,128)S(1)}, f32[2,512,6]{2,1,0:T(8,128)S(1)}, u32[]{:S(2)}, u32[]{:S(2)}) %collective-permute-start.4) | collective-permute-done | bytes 24608 | tf_op jit(solution)/shard_map/ppermute | solution.py:27
  133.1 1.3 collective-permute-start.7
  134.4 4.9 %collective-permute-start.6 = (f32[2,6,140]{2,1,0:T(8,128)S(1)}, f32[2,6,140]{2,1,0:T(8,128)S(1)}, u32[]{:S(2)}, u32[]{:S(2)}) collective-permute-start(f32[2,6,140]{2,1,0:T(8,128)S(1)} %get-tuple-element.66), channel_id=1, source_target_pairs={{0,1},{1,2},{2,3},{4,5},{5,6},{6,7},{8,9},{9,10},{10,11},{12,13},{... | collective-permute-start | bytes 20168 | tf_op jit(solution)/shard_map/ppermute | solution.py:27
  139.3 1.4 collective-permute-done.6
  149.3 1.2 fusion.24
  152.9 40.7 %shard_map.92 = f32[6,512,128]{2,1,0:T(8,128)S(1)} custom-call(f32[6,512,128]{2,1,0:T(8,128)S(1)} %broadcast_multiply_fusion.x_ref, f32[384,128]{1,0:T(8,128)S(1)} %fusion.193.taps_ref), custom_call_target="tpu_custom_call" | custom-call | flops 1811939328 | bytes 3145728 | tf_op jit(solution)/shard_map/pallas_call | solution.py:202
  193.7 1.3 add.288
  (95 shorter events, 25.2 us)
Async XLA Ops:
  1.4 1.4 copy-start
  2.8 42.0 %copy-start.11 = (f32[6]{0:T(128)S(1)}, f32[6]{0:T(128)}, u32[]{:S(2)}) copy-start(f32[6]{0:T(128)} %param.10) | copy-start | bytes 76
  44.8 1.0 copy-start.2
  44.8 1.0 copy-start.4
  50.8 6.9 %copy-start.9 = (s32[1,32,8]{1,2,0:T(8,128)S(1)}, s32[1,32,8]{1,2,0:T(8,128)}, u32[]{:S(2)}) copy-start(s32[1,32,8]{1,2,0:T(8,128)} %param.14) | copy-start | bytes 3076
  50.9 7.0 %copy-start.12 = (s32[1,32]{1,0:T(1,128)S(1)}, s32[1,32]{1,0:T(1,128)}, u32[]{:S(2)}) copy-start(s32[1,32]{1,0:T(1,128)} %param.15) | copy-start | bytes 388
  50.9 7.1 %copy-start.7 = (f32[1,32,8,128]{3,2,1,0:T(8,128)S(1)}, f32[1,32,8,128]{3,2,1,0:T(8,128)}, u32[]{:S(2)}) copy-start(f32[1,32,8,128]{3,2,1,0:T(8,128)} %param.16) | copy-start | bytes 393220
  50.9 13.1 %collective-permute-start.1 = (f32[8,512,6]{1,0,2:T(8,128)S(1)}, f32[8,512,6]{1,0,2:T(8,128)S(1)}, u32[]{:S(2)}, u32[]{:S(2)}) collective-permute-start(f32[8,512,6]{1,0,2:T(8,128)S(1)} %copy.31), channel_id=1, source_target_pairs={{4,0},{8,4},{12,8},{16,12},{20,16},{24,20},{28,24},{5,1},{9,5},{13... | collective-permute-start | bytes 294920 | tf_op jit(solution)/shard_map/ppermute | solution.py:30
  55.8 10.2 %collective-permute-start = (f32[8,512,6]{1,0,2:T(8,128)S(1)}, f32[8,512,6]{1,0,2:T(8,128)S(1)}, u32[]{:S(2)}, u32[]{:S(2)}) collective-permute-start(f32[8,512,6]{1,0,2:T(8,128)S(1)} %copy.30), channel_id=1, source_target_pairs={{0,4},{4,8},{8,12},{12,16},{16,20},{20,24},{24,28},{1,5},{5,9},{9,... | collective-permute-start | bytes 294920 | tf_op jit(solution)/shard_map/ppermute | solution.py:27
  58.6 52.8 %all-to-all-start = ((f32[32,9,128]{2,1,0:T(8,128)}), f32[32,9,128]{2,1,0:T(8,128)}, u32[]{:S(2)}, u32[]{:S(2)}) async-start(f32[32,9,128]{2,1,0:T(8,128)} %pad_maximum_fusion.13), calls=%async_computation | async-start | bytes 524288 | tf_op jit(solution)/shard_map/all_to_all | solution.py:235
  66.0 2.0 %copy-start.3 = (f32[512,128]{1,0:T(8,128)S(1)}, f32[512,128]{1,0:T(8,128)}, u32[]{:S(2)}) copy-start(f32[512,128]{1,0:T(8,128)} %param.12) | copy-start | bytes 786436
  66.0 2.0 %copy-start.5 = (f32[512,128]{1,0:T(8,128)S(1)}, f32[512,128]{1,0:T(8,128)}, u32[]{:S(2)}) copy-start(f32[512,128]{1,0:T(8,128)} %param.11) | copy-start | bytes 786436
  69.0 7.0 %copy-start.10 = (s32[1,32,8]{1,2,0:T(8,128)S(1)}, s32[1,32,8]{1,2,0:T(8,128)}, u32[]{:S(2)}) copy-start(s32[1,32,8]{1,2,0:T(8,128)} %param.13) | copy-start | bytes 3076
  69.0 7.2 %collective-permute-start.3 = (f32[8,6,140]{2,1,0:T(8,128)S(1)}, f32[8,6,140]{2,1,0:T(8,128)S(1)}, u32[]{:S(2)}, u32[]{:S(2)}) collective-permute-start(f32[8,6,140]{2,1,0:T(8,128)S(1)} %get-tuple-element.28), channel_id=1, source_target_pairs={{1,0},{2,1},{3,2},{5,4},{6,5},{7,6},{9,8},{10,9},{11,10},{13,12},{... | collective-permute-start | bytes 80648 | tf_op jit(solution)/shard_map/ppermute | solution.py:30
  70.3 6.4 %collective-permute-start.2 = (f32[8,6,140]{2,1,0:T(8,128)S(1)}, f32[8,6,140]{2,1,0:T(8,128)S(1)}, u32[]{:S(2)}, u32[]{:S(2)}) collective-permute-start(f32[8,6,140]{2,1,0:T(8,128)S(1)} %get-tuple-element.27), channel_id=1, source_target_pairs={{0,1},{1,2},{2,3},{4,5},{5,6},{6,7},{8,9},{9,10},{10,11},{12,13},{... | collective-permute-start | bytes 80648 | tf_op jit(solution)/shard_map/ppermute | solution.py:27
  109.5 1.6 copy-start.6
  111.0 3.5 %copy-start.8 = (f32[2,128,128]{2,1,0:T(8,128)S(1)}, f32[2,128,128]{2,1,0:T(8,128)}, u32[]{:S(2)}) copy-start(f32[2,128,128]{2,1,0:T(8,128)} %param.17) | copy-start | bytes 393220
  116.8 11.6 %collective-permute-start.5 = (f32[2,512,6]{2,1,0:T(8,128)S(1)}, f32[2,512,6]{2,1,0:T(8,128)S(1)}, u32[]{:S(2)}, u32[]{:S(2)}) collective-permute-start(f32[2,512,6]{2,1,0:T(8,128)S(1)} %get-tuple-element.91), channel_id=1, source_target_pairs={{4,0},{8,4},{12,8},{16,12},{20,16},{24,20},{28,24},{5,1},{9,5},{13... | collective-permute-start | bytes 73736 | tf_op jit(solution)/shard_map/ppermute | solution.py:30
  118.9 14.1 %collective-permute-start.4 = (f32[2,512,6]{2,1,0:T(8,128)S(1)}, f32[2,512,6]{2,1,0:T(8,128)S(1)}, u32[]{:S(2)}, u32[]{:S(2)}) collective-permute-start(f32[2,512,6]{2,1,0:T(8,128)S(1)} %get-tuple-element.90), channel_id=1, source_target_pairs={{0,4},{4,8},{8,12},{12,16},{16,20},{20,24},{24,28},{1,5},{5,9},{9,... | collective-permute-start | bytes 73736 | tf_op jit(solution)/shard_map/ppermute | solution.py:27
  133.1 6.2 %collective-permute-start.7 = (f32[2,6,140]{2,1,0:T(8,128)S(1)}, f32[2,6,140]{2,1,0:T(8,128)S(1)}, u32[]{:S(2)}, u32[]{:S(2)}) collective-permute-start(f32[2,6,140]{2,1,0:T(8,128)S(1)} %get-tuple-element.67), channel_id=1, source_target_pairs={{1,0},{2,1},{3,2},{5,4},{6,5},{7,6},{9,8},{10,9},{11,10},{13,12},{... | collective-permute-start | bytes 20168 | tf_op jit(solution)/shard_map/ppermute | solution.py:30
  134.4 6.3 %collective-permute-start.6 = (f32[2,6,140]{2,1,0:T(8,128)S(1)}, f32[2,6,140]{2,1,0:T(8,128)S(1)}, u32[]{:S(2)}, u32[]{:S(2)}) collective-permute-start(f32[2,6,140]{2,1,0:T(8,128)S(1)} %get-tuple-element.66), channel_id=1, source_target_pairs={{0,1},{1,2},{2,3},{4,5},{5,6},{6,7},{8,9},{9,10},{10,11},{12,13},{... | collective-permute-start | bytes 20168 | tf_op jit(solution)/shard_map/ppermute | solution.py:27
  152.9 40.8 %copy-start.1 = (f32[6,512,128]{2,1,0:T(8,128)S(1)}, f32[6,512,128]{2,1,0:T(8,128)}, u32[]{:S(2)}) copy-start(f32[6,512,128]{2,1,0:T(8,128)} %x_ref.1) | copy-start | bytes 4718596
where the time goes:
time: 196 us; the launch traced here: 195 us
  Pallas kernels  82.7 us (42%)
  other arithmetic  49.8 us (25%)
  starting transfers between devices  26.3 us (13%)
  local copies, waits for them, and re-layouts  17.6 us (9%)
  waiting for transfers between devices  13.8 us (7%)
  matrix products  3.64 us (2%)
    pallas_call x2, Pallas kernels, correlate(): pl.pallas_call(functools.partial(correlate_kernel, counts), out_shape=jax...  82.7 us
    sub x4, other arithmetic, laplace(): padded[:, 2:, 1:-1] + padded[:, :-2, 1:-1] + padded[:, 1:-1, 2:]  17.3 us
    ppermute x4, starting transfers between devices, with_halo(): lax.ppermute(lax.slice_in_dim(block, block.shape[dim] - width, None, axis...  13.7 us
    ppermute x4, starting transfers between devices, with_halo(): lax.ppermute(lax.slice_in_dim(block, 0, width, axis=dim), axis, backward)  7.32 us
    ppermute x4, waiting for transfers between devices, with_halo(): lax.ppermute(lax.slice_in_dim(block, 0, width, axis=dim), axis, backward)  7.24 us
    ppermute x4, waiting for transfers between devices, with_halo(): lax.ppermute(lax.slice_in_dim(block, block.shape[dim] - width, None, axis...  6.53 us
    concatenate x2, other arithmetic, with_halo(): block = jnp.concatenate([low, block, high], axis=dim)  6.08 us
    all_to_all x1, starting transfers between devices, observation_sums(): lax.all_to_all(sent, ('gx', 'gy'), split_axis=0, concat_axis=0, tiled=True)  5.3 us
  transfers between devices with their start and end apart: 9, of which 4 were waited for; matrix products, arithmetic and copies ran while one was open for 23% of the time, Pallas kernels for 0%

commit v1 on v0

--- a/solution.py
+++ b/solution.py
@@ -17,19 +17,6 @@
 FRICTION = 0.5
 DIFFUSION = (0.4, 0.25)
 SETTLING = (0.5, 0.2)
-
-
-def with_halo(block, sides, width):
-    for axis, dim in sides:
-        count = lax.axis_size(axis)
-        forward = [(i, i + 1) for i in range(count - 1)]
-        backward = [(target, source) for source, target in forward]
-        low = lax.ppermute(
-            lax.slice_in_dim(block, block.shape[dim] - width, None, axis=dim), axis, forward
-        )
-        high = lax.ppermute(lax.slice_in_dim(block, 0, width, axis=dim), axis, backward)
-        block = jnp.concatenate([low, block, high], axis=dim)
-    return block
 
 
 def band_table():
@@ -220,7 +207,7 @@
         ),
         cost_estimate=pl.CostEstimate(
             flops=36 * fields * rows * cols * HALF,
-            bytes_accessed=8 * fields * rows * cols,
+            bytes_accessed=256 * fields * rows * cols,
             transcendentals=0,
         ),
     )(block, kernel)
@@ -248,145 +235,255 @@
     return sums
 
 
-def slope_x(padded):
-    return 0.5 * (padded[:, 1:-1, 2:] - padded[:, 1:-1, :-2])
-
-
-def slope_y(padded):
-    return 0.5 * (padded[:, 2:, 1:-1] - padded[:, :-2, 1:-1])
-
-
-def laplace(padded):
-    return (
-        padded[:, 2:, 1:-1]
-        + padded[:, :-2, 1:-1]
-        + padded[:, 1:-1, 2:]
-        + padded[:, 1:-1, :-2]
-        - 4.0 * padded[:, 1:-1, 1:-1]
-    )
-
-
-def inside_grid(margin, rows, cols):
-    row_ids = lax.axis_index("gy") * rows + jnp.arange(rows + 2 * margin, dtype=jnp.int32) - margin
-    col_ids = lax.axis_index("gx") * cols + jnp.arange(cols + 2 * margin, dtype=jnp.int32) - margin
-    row_ok = (row_ids >= 0) & (row_ids < rows * lax.axis_size("gy"))
-    col_ok = (col_ids >= 0) & (col_ids < cols * lax.axis_size("gx"))
-    return (row_ok[:, None] & col_ok[None, :]).astype(jnp.float32)
-
-
-def trim(plane):
-    return plane[1:-1, 1:-1]
-
-
-def trim_two(plane):
-    return plane[2:-2, 2:-2]
-
-
-def region_step(fields, depth, mobility, inside):
-    height, speed_x, speed_y, bed_level, silt_one, silt_two = (
-        fields[0],
-        fields[1],
-        fields[2],
-        fields[3],
-        fields[4],
-        fields[5],
-    )
-    fluxes = jnp.stack(
-        [
-            depth * speed_x,
-            depth * speed_y,
-            mobility * speed_x,
-            mobility * speed_y,
-            silt_one,
-            silt_two,
-        ]
-    )
-    along_x = slope_x(fluxes[:4])
-    along_y = slope_y(fluxes[:4])
-    spread = laplace(fluxes[4:])
-    middle = trim(inside)
-    height_new = (trim(height) - TIME_STEP * (along_x[0] + along_y[1])) * middle
-    bed_new = (
-        trim(bed_level)
-        - TIME_STEP * (along_x[2] + along_y[3])
-        + TIME_STEP * (SETTLING[0] * trim(silt_one) + SETTLING[1] * trim(silt_two))
-    ) * middle
-    silt_one_new = (
-        trim(silt_one)
-        + TIME_STEP * DIFFUSION[0] * spread[0]
-        - TIME_STEP * SETTLING[0] * trim(silt_one)
-    ) * middle
-    silt_two_new = (
-        trim(silt_two)
-        + TIME_STEP * DIFFUSION[1] * spread[1]
-        - TIME_STEP * SETTLING[1] * trim(silt_two)
-    ) * middle
-    surface = (height_new + bed_new)[None]
-    core = trim_two(inside)
-    speed_x_new = (
-        (1.0 - TIME_STEP * FRICTION) * trim_two(speed_x) - TIME_STEP * GRAVITY * slope_x(surface)[0]
-    ) * core
-    speed_y_new = (
-        (1.0 - TIME_STEP * FRICTION) * trim_two(speed_y) - TIME_STEP * GRAVITY * slope_y(surface)[0]
-    ) * core
-    return jnp.stack(
-        [
-            trim(height_new),
-            speed_x_new,
-            speed_y_new,
-            trim(bed_new),
-            trim(silt_one_new),
-            trim(silt_two_new),
-        ]
-    )
-
-
-def region_adjoint(adjoint, depth, mobility, inside):
-    adj_height, adj_speed_x, adj_speed_y, adj_bed, adj_silt_one, adj_silt_two = (
-        adjoint[0],
-        adjoint[1],
-        adjoint[2],
-        adjoint[3],
-        adjoint[4],
-        adjoint[5],
-    )
-    adj_surface = (
-        TIME_STEP * GRAVITY * (slope_x(adj_speed_x[None])[0] + slope_y(adj_speed_y[None])[0])
-    )
-    middle = trim(inside)
-    height_mid = (trim(adj_height) + adj_surface) * middle
-    bed_mid = (trim(adj_bed) + adj_surface) * middle
-    levels = jnp.stack([height_mid, bed_mid, trim(adj_silt_one), trim(adj_silt_two)])
-    grad_x = TIME_STEP * slope_x(levels[:2])
-    grad_y = TIME_STEP * slope_y(levels[:2])
-    spread = laplace(levels[2:])
-    core = trim_two(inside)
-    bed_core = trim(bed_mid)
-    new_speed_x = (
-        (1.0 - TIME_STEP * FRICTION) * trim_two(adj_speed_x)
-        + trim_two(depth) * grad_x[0]
-        + trim_two(mobility) * grad_x[1]
-    ) * core
-    new_speed_y = (
-        (1.0 - TIME_STEP * FRICTION) * trim_two(adj_speed_y)
-        + trim_two(depth) * grad_y[0]
-        + trim_two(mobility) * grad_y[1]
-    ) * core
-    new_silt_one = (
-        trim_two(adj_silt_one)
-        + TIME_STEP * DIFFUSION[0] * spread[0]
-        - TIME_STEP * SETTLING[0] * trim_two(adj_silt_one)
-        + TIME_STEP * SETTLING[0] * bed_core
-    ) * core
-    new_silt_two = (
-        trim_two(adj_silt_two)
-        + TIME_STEP * DIFFUSION[1] * spread[1]
-        - TIME_STEP * SETTLING[1] * trim_two(adj_silt_two)
-        + TIME_STEP * SETTLING[1] * bed_core
-    ) * core
-    return jnp.stack(
-        [trim(height_mid), new_speed_x, new_speed_y, bed_core, new_silt_one, new_silt_two]
-    )
+CHUNK = 32
+REACH = 8
+PLANES = (0, 3, 1, 2, 4, 5)
+
+
+def flow_kernel(
+    counts, x_ref, scale_ref, depth_ref, mobility_ref, seen_ref, sums_ref, precision_ref, out_ref,
+    st, pack, got, landed, send, recv,
+):
+    _, rows, cols = x_ref.shape
+    width = 2 * cols
+    around = neighbours(("gx", "gy"), counts)
+    greet(around)
+    base = CHUNK
+    row_low, col_low = lax.axis_index("gy") * rows, lax.axis_index("gx") * cols
+
+    def start(row):
+        return pl.ds(pl.multiple_of(row, 8), CHUNK)
+
+    for there, spot in ((around[0][2], 0), (around[1][2], 1)):
+
+        @pl.when(jnp.logical_not(there))
+        def _():
+            for phase in range(2):
+                got[phase, spot] = jnp.zeros((rows, cols), jnp.float32)
+
+    def copy(phase, side):
+        axis, other, _ = around[side]
+        planes = 8 if phase == 0 else 2
+        if side == 0:
+            source, target = pack.at[phase, 0], got.at[phase, 1]
+        elif side == 1:
+            source, target = pack.at[phase, 1], got.at[phase, 0]
+        elif side == 2:
+            source = st.at[pl.ds(0, planes), pl.ds(base, REACH)]
+            target = landed.at[phase, 1, pl.ds(0, planes)]
+        else:
+            source = st.at[pl.ds(0, planes), pl.ds(base + rows - REACH, REACH)]
+            target = landed.at[phase, 0, pl.ds(0, planes)]
+        return pltpu.make_async_remote_copy(
+            src_ref=source,
+            dst_ref=target,
+            send_sem=send.at[phase, side],
+            recv_sem=recv.at[phase, side],
+            device_id={axis: other},
+            device_id_type=pl.DeviceIdType.MESH,
+        )
+
+    def each(phase, sides, act):
+        for side, way in sides:
+
+            @pl.when(around[side][2])
+            def _():
+                act(copy(phase, way))
+
+    def exchange(phase):
+        planes = 8 if phase == 0 else 2
+        lane = lax.broadcasted_iota(jnp.int32, (CHUNK, cols), 1)
+
+        def fill(i, carry):
+            to_low = jnp.zeros((CHUNK, cols), jnp.float32)
+            to_high = to_low
+            for p in range(planes):
+                block = st[p, start(base + i * CHUNK), 0:cols]
+                here = (lane >= REACH * p) & (lane < REACH * (p + 1))
+                first = block if p == 0 else pltpu.roll(block, REACH * p, 1)
+                to_low = jnp.where(here, first, to_low)
+                to_high = jnp.where(here, pltpu.roll(block, REACH * p + REACH, 1), to_high)
+            pack[phase, 0, start(i * CHUNK), :] = to_low
+            pack[phase, 1, start(i * CHUNK), :] = to_high
+            return carry
+
+        lax.fori_loop(0, rows // CHUNK, fill, 0)
+        each(phase, ((0, 0), (1, 1)), lambda c: c.start())
+        each(phase, ((0, 1), (1, 0)), lambda c: c.wait_recv())
+
+        def spread(i, carry):
+            from_low = got[phase, 0, start(i * CHUNK), :]
+            from_high = got[phase, 1, start(i * CHUNK), :]
+            for p in range(planes):
+                high = from_high if p == 0 else pltpu.roll(from_high, cols - REACH * p, 1)
+                low = pltpu.roll(from_low, cols - REACH - REACH * p, 1)
+                st[p, start(base + i * CHUNK), cols:width] = jnp.where(
+                    lane < REACH, high, jnp.where(lane >= cols - REACH, low, 0.0)
+                )
+            return carry
+
+        lax.fori_loop(0, rows // CHUNK, spread, 0)
+        each(phase, ((2, 2), (3, 3)), lambda c: c.start())
+        each(phase, ((2, 3), (3, 2)), lambda c: c.wait_recv())
+
+        @pl.when(around[2][2])
+        def _():
+            for p in range(planes):
+                st[p, pl.ds(base - REACH, REACH), :] = landed[phase, 0, p]
+
+        @pl.when(around[3][2])
+        def _():
+            for p in range(planes):
+                st[p, pl.ds(base + rows, REACH), :] = landed[phase, 1, p]
+
+        each(phase, ((0, 0), (1, 1), (2, 2), (3, 3)), lambda c: c.wait_send())
+
+    def sweep(body):
+        def one(i, carry):
+            row = CHUNK // 2 + i * CHUNK
+            row_id = lax.broadcasted_iota(jnp.int32, (CHUNK, width), 0) + (row - base + row_low)
+            lane = lax.broadcasted_iota(jnp.int32, (CHUNK, width), 1)
+            col_id = jnp.where(lane < cols + cols // 2, lane, lane - width) + col_low
+            inside = (
+                (row_id >= 0)
+                & (row_id < rows * counts[1])
+                & (col_id >= 0)
+                & (col_id < cols * counts[0])
+            )
+
+            def mid(p):
+                return st[p, start(row), :]
+
+            def tall(p):
+                return st[p, pl.ds(pl.multiple_of(row - 8, 8), CHUNK + 16), :]
+
+            def put(p, value):
+                st[p, start(row), :] = jnp.where(inside, value, 0.0)
+
+            body(mid, tall, put)
+            return carry
+
+        lax.fori_loop(0, (rows + CHUNK) // CHUNK, one, 0)
+
+    def dx(value):
+        return 0.5 * (pltpu.roll(value, width - 1, 1) - pltpu.roll(value, 1, 1))
+
+    def dy(window):
+        return 0.5 * (window[9 : 9 + CHUNK] - window[7 : 7 + CHUNK])
+
+    def lap(window):
+        value = window[8 : 8 + CHUNK]
+        return (
+            window[9 : 9 + CHUNK]
+            + window[7 : 7 + CHUNK]
+            + pltpu.roll(value, width - 1, 1)
+            + pltpu.roll(value, 1, 1)
+            - 4.0 * value
+        )
+
+    def silt(now, j, tall):
+        window = tall(now + j)
+        value = window[8 : 8 + CHUNK]
+        return value, (
+            value
+            + TIME_STEP * DIFFUSION[j] * lap(window)
+            - TIME_STEP * SETTLING[j] * value
+        )
+
+    for p in range(10):
+        st[p] = jnp.zeros(st.shape[1:], jnp.float32)
+    inner = pl.ds(base, rows)
+    for p, field in enumerate(PLANES):
+        st[p, inner, 0:cols] = scale_ref[field] * x_ref[field]
+    st[6, inner, 0:cols] = depth_ref[...]
+    st[7, inner, 0:cols] = mobility_ref[...]
+    exchange(0)
+
+    keep = 1.0 - TIME_STEP * FRICTION
+    where_silt = (4, 8)
+    for step in range(STEPS):
+        now, later = where_silt[step % 2], where_silt[(step + 1) % 2]
+
+        def levels(mid, tall, put):
+            u, v, depth, mobility = tall(2), tall(3), tall(6), tall(7)
+            part = slice(8, 8 + CHUNK)
+            flow = dx(depth[part] * u[part]) + dy(depth * v)
+            load = dx(mobility[part] * u[part]) + dy(mobility * v)
+            one, one_new = silt(now, 0, tall)
+            two, two_new = silt(now, 1, tall)
+            put(0, mid(0) - TIME_STEP * flow)
+            put(1, mid(1) - TIME_STEP * load + TIME_STEP * (SETTLING[0] * one + SETTLING[1] * two))
+            put(later, one_new)
+            put(later + 1, two_new)
+
+        def speeds(mid, tall, put):
+            surface = tall(0) + tall(1)
+            put(2, keep * mid(2) - TIME_STEP * GRAVITY * dx(surface[8 : 8 + CHUNK]))
+            put(3, keep * mid(3) - TIME_STEP * GRAVITY * dy(surface))
+
+        sweep(levels)
+        if step < STEPS - 1:
+            sweep(speeds)
+
+    height, bed = st[0, inner, 0:cols], st[1, inner, 0:cols]
+    sar = seen_ref[0] * (height + bed) - sums_ref[0]
+    lidar = seen_ref[1] * bed - sums_ref[1]
+    sar = mul_pair(split(sar), split(precision_ref[0]))
+    lidar = mul_pair(split(lidar), split(precision_ref[1]))
+    for p in range(6):
+        st[p] = jnp.zeros(st.shape[1:], jnp.float32)
+    st[0, inner, 0:cols] = sar
+    st[1, inner, 0:cols] = sar + lidar
+    exchange(1)
+
+    for step in range(STEPS):
+        now, later = where_silt[step % 2], where_silt[(step + 1) % 2]
+
+        def adj_levels(mid, tall, put):
+            surface = TIME_STEP * GRAVITY * (dx(mid(2)) + dy(tall(3)))
+            put(0, mid(0) + surface)
+            put(1, mid(1) + surface)
+
+        def adj_speeds(mid, tall, put):
+            height, bed, depth, mobility = tall(0), tall(1), mid(6), mid(7)
+            part = slice(8, 8 + CHUNK)
+            put(2, keep * mid(2) + TIME_STEP * (depth * dx(height[part]) + mobility * dx(bed[part])))
+            put(3, keep * mid(3) + TIME_STEP * (depth * dy(height) + mobility * dy(bed)))
+            for j in range(2):
+                _, new = silt(now, j, tall)
+                put(later + j, new + TIME_STEP * SETTLING[j] * bed[part])
+
+        if step > 0:
+            sweep(adj_levels)
+        sweep(adj_speeds)
+
+    last = where_silt[STEPS % 2]
+    for p, field in enumerate(PLANES):
+        q = p if p < 4 else last + p - 4
+        out_ref[field] = scale_ref[field] * st[q, inner, 0:cols]
+
+
+def flow(block, field_scale, depth, mobility, seen, sums, obs_precision):
+    _, rows, cols = block.shape
+    counts = (lax.axis_size("gx"), lax.axis_size("gy"))
+    full = pl.BlockSpec(memory_space=pltpu.VMEM)
+    return pl.pallas_call(
+        functools.partial(flow_kernel, counts),
+        out_shape=jax.ShapeDtypeStruct(block.shape, jnp.float32),
+        in_specs=[full, pl.BlockSpec(memory_space=pltpu.SMEM)] + [full] * 5,
+        out_specs=full,
+        scratch_shapes=[
+            pltpu.VMEM((10, rows + 2 * CHUNK, 2 * cols), jnp.float32),
+            pltpu.VMEM((2, 2, rows, cols), jnp.float32),
+            pltpu.VMEM((2, 2, rows, cols), jnp.float32),
+            pltpu.VMEM((2, 2, 8, REACH, 2 * cols), jnp.float32),
+            pltpu.SemaphoreType.DMA((2, 4)),
+            pltpu.SemaphoreType.DMA((2, 4)),
+        ],
+        compiler_params=pltpu.CompilerParams(
+            collective_id=3, has_side_effects=True, vmem_limit_bytes=40 * 2**20
+        ),
+    )(block, field_scale, depth, mobility, seen, sums, obs_precision)
 
 
 def on_device(
@@ -401,51 +498,17 @@
     obs_precision,
 ):
     kernel = band_table()
-    scales = field_scale[:, None, None]
     rows = water_depth.shape[0]
-    cols = water_depth.shape[1]
     (count_sar, sum_sar), (count_lidar, sum_lidar) = observation_sums(
         rows, footprint[0], instrument[0], live_counts[0], observed[0]
     )
-    fields = scales * correlate(control, kernel, 1)
-    margin = 2 * STEPS
-    stacked = jnp.concatenate([fields, water_depth[None], bed_mobility[None]])
-    extended = with_halo(stacked, (("gx", 2), ("gy", 1)), margin)
-    depth_wide = extended[6]
-    mobility_wide = extended[7]
-    inside_wide = inside_grid(margin, rows, cols)
-    fields = extended[:6]
-    depth_now, mobility_now, inside_now = (depth_wide, mobility_wide, inside_wide)
-    for _ in range(STEPS):
-        fields = region_step(fields, depth_now, mobility_now, inside_now)
-        depth_now, mobility_now, inside_now = (
-            trim_two(depth_now),
-            trim_two(mobility_now),
-            trim_two(inside_now),
-        )
-    misfit_sar = count_sar * (fields[0] + fields[3]) - sum_sar
-    misfit_lidar = count_lidar * fields[3] - sum_lidar
-    weighted_sar = jnp.einsum(
-        "rj,ij->ri", misfit_sar, obs_precision[0], precision=lax.Precision.HIGHEST
+    seen = jnp.broadcast_to(jnp.stack([count_sar, count_lidar]), (2,) + water_depth.shape)
+    sums = jnp.stack([sum_sar, sum_lidar])
+    smooth = correlate(control, kernel, 1)
+    adjoint = flow(
+        smooth, field_scale, water_depth, bed_mobility, seen, sums, obs_precision
     )
-    weighted_lidar = jnp.einsum(
-        "rj,ij->ri", misfit_lidar, obs_precision[1], precision=lax.Precision.HIGHEST
-    )
-    planes = jnp.stack([weighted_sar, weighted_sar + weighted_lidar])
-    wide_planes = with_halo(planes, (("gx", 2), ("gy", 1)), margin)
-    empty_plane = jnp.zeros_like(wide_planes[0])
-    adjoint = jnp.stack(
-        [wide_planes[0], empty_plane, empty_plane, wide_planes[1], empty_plane, empty_plane]
-    )
-    depth_now, mobility_now, inside_now = (depth_wide, mobility_wide, inside_wide)
-    for _ in range(STEPS):
-        adjoint = region_adjoint(adjoint, depth_now, mobility_now, inside_now)
-        depth_now, mobility_now, inside_now = (
-            trim_two(depth_now),
-            trim_two(mobility_now),
-            trim_two(inside_now),
-        )
-    return control + correlate(scales * adjoint, kernel, 2)
+    return control + correlate(adjoint, kernel, 2)
 
 
 def solution(mesh):

time: 196 us -> 159 us (0.81)
  Pallas kernels: 82.7 us -> 142 us
  other arithmetic: 49.8 us -> 4.85 us
  starting transfers between devices: 26.3 us -> 6.1 us
  local copies, waits for them, and re-layouts: 17.6 us -> 3.44 us
  waiting for transfers between devices: 13.8 us -> 0.01 us
  matrix products: 3.64 us -> 0.8 us
    pallas_call x0 -> x1, Pallas kernels: none -> 59.3 us  [flow(): pl.pallas_call(functools.partial(flow_kernel, counts), out_shape=jax.Shap...]
    ppermute x8 -> x0, starting transfers between devices: 21 us -> none  [the longest x4 13.7 us: with_halo(): lax.ppermute(lax.slice_in_dim(block, block.shape[dim] - width, None, axis...]
    sub x6 -> x0, other arithmetic: 18 us -> none  [the longest x4 17.3 us: laplace(): padded[:, 2:, 1:-1] + padded[:, :-2, 1:-1] + padded[:, 1:-1, 2:]]
    mul x20 -> x0, other arithmetic: 14.4 us -> none  [the longest x3 5.25 us: slope_x(): return 0.5 * (padded[:, 1:-1, 2:] - padded[:, 1:-1, :-2])]
    ppermute x8 -> x0, waiting for transfers between devices: 13.8 us -> none  [the longest x4 7.24 us: with_halo(): lax.ppermute(lax.slice_in_dim(block, 0, width, axis=dim), axis, backward)]
    slice x6 -> x0, local copies, waits for them, and re-layouts: 9.3 us -> none  [the longest x2 4.86 us: with_halo(): lax.slice_in_dim(block, block.shape[dim] - width, None, axis=dim)]
    concatenate x3 -> x0, other arithmetic: 6.23 us -> none  [the longest x2 6.08 us: with_halo(): block = jnp.concatenate([low, block, high], axis=dim)]
    ppermute x2 -> x0, local copies, waits for them, and re-layouts: 4.02 us -> none  [the longest x1 2.02 us: with_halo(): lax.ppermute(lax.slice_in_dim(block, 0, width, axis=dim), axis, backward)]
  transfers between devices with their start and end apart: 9 -> 1, of which waited for: 4 -> 0; matrix products, arithmetic and copies ran while one was open for 23% -> 1% of each run, Pallas kernels for 0% -> 27%
where the time goes in v1:
time: 159 us; the launch traced here: 158 us
  Pallas kernels  142 us (89%)
  starting transfers between devices  6.1 us (4%)
  other arithmetic  4.85 us (3%)
  local copies, waits for them, and re-layouts  3.44 us (2%)
    pallas_call x2, Pallas kernels, correlate(): pl.pallas_call(functools.partial(correlate_kernel, counts), out_shape=jax...  83 us
    pallas_call x1, Pallas kernels, flow(): pl.pallas_call(functools.partial(flow_kernel, counts), out_shape=jax.Shap...  59.3 us
    all_to_all x1, starting transfers between devices, observation_sums(): lax.all_to_all(sent, ('gx', 'gy'), split_axis=0, concat_axis=0, tiled=True)  6.1 us
  transfers between devices with their start and end apart: 1, of which 0 were waited for; matrix products, arithmetic and copies ran while one was open for 1% of the time, Pallas kernels for 27%

profile of v1, /device:TPU:4, one launch (start us, length us, event | category | flops | bytes accessed | tf_op | source)
XLA Modules:
  0.0 158.5 jit_solution(10594870823894548658)
XLA Ops:
  0.0 0.8 copy.14
  0.8 0.7 fusion.12
  1.5 1.6 %pad_maximum_fusion.1 = f32[32,9,128]{2,1,0:T(8,128)} fusion(f32[32,1,128]{2,1,0:T(1,128)S(1)} %bitcast.20, f32[32,8,128]{2,1,0:T(8,128)} %bitcast.19), kind=kLoop, calls=%fused_computation.9 | loop fusion | flops 36864 | bytes 294912 | tf_op jit(solution)/shard_map/concatenate | solution.py:221
  3.1 6.1 %all-to-all-start = ((f32[32,9,128]{2,1,0:T(8,128)}), f32[32,9,128]{2,1,0:T(8,128)S(1)}, u32[]{:S(2)}, u32[]{:S(2)}) async-start(f32[32,9,128]{2,1,0:T(8,128)} %pad_maximum_fusion.1), calls=%async_computation | async-start | bytes 524288 | tf_op jit(solution)/shard_map/all_to_all | solution.py:222
  9.2 0.7 fusion.15
  10.7 0.8 copy.13
  11.4 0.1 eq.41
  11.5 0.1 fusion.11.taps_ref
  11.6 0.0 copy-start
  11.6 1.4 copy-done
  13.0 42.3 %shard_map.91.x_ref = f32[6,512,128]{2,1,0:T(8,128)S(1)} custom-call(f32[6,512,128]{2,1,0:T(8,128)S(1)} %copy-done, f32[384,128]{1,0:T(8,128)S(1)} %fusion.11.taps_ref), custom_call_target="tpu_custom_call" | custom-call | flops 1811939328 | bytes 100663296 | tf_op jit(solution)/shard_map/pallas_call | solution.py:189
  55.3 0.0 copy-start.2
  55.3 0.0 copy-start.3
  55.3 0.0 copy-start.4
  55.3 0.0 copy-start.5
  55.3 0.0 all-to-all-done
  55.4 0.1 compare_reduce_fusion.1
  55.5 0.1 eq.47
  55.6 0.1 eq.50
  55.7 0.3 convert_reduce_fusion.1
  55.9 0.4 convolution_bitcast_fusion.1
  56.3 0.4 convolution_bitcast_fusion
  56.8 0.2 broadcast_in_dim.28.seen_ref
  57.0 0.0 copy-done.2
  57.0 0.0 copy-done.3
  57.0 0.0 copy-done.4
  57.0 0.0 copy-done.5
  57.0 59.3 %shard_map.92.x_ref = f32[6,512,128]{2,1,0:T(8,128)S(1)} custom-call(f32[6,512,128]{2,1,0:T(8,128)S(1)} %shard_map.91.x_ref, f32[6]{0:T(128)S(1)} %copy-done.5, f32[512,128]{1,0:T(8,128)S(1)} %copy-done.2, f32[512,128]{1,0:T(8,128)S(1)} %copy-done.3, f32[2,512,128]{2,1,0:T(8,128)S(1)} %broadcast_in_dim.28.seen_ref, ...), custom_call_target="tpu_custom_call" | custom-call | tf_op jit(solution)/shard_map/pallas_call | solution.py:470
  116.4 0.0 copy-start.1
  116.4 40.8 %shard_map.93 = f32[6,512,128]{2,1,0:T(8,128)S(1)} custom-call(f32[6,512,128]{2,1,0:T(8,128)S(1)} %shard_map.92.x_ref, f32[384,128]{1,0:T(8,128)S(1)} %fusion.11.taps_ref), custom_call_target="tpu_custom_call" | custom-call | flops 1811939328 | bytes 100663296 | tf_op jit(solution)/shard_map/pallas_call | solution.py:189
  157.2 0.0 copy-done.1
  157.2 1.3 add.26
  (3 shorter events, 0.1 us)
Async XLA Ops:
  3.1 52.2 %all-to-all-start = ((f32[32,9,128]{2,1,0:T(8,128)}), f32[32,9,128]{2,1,0:T(8,128)S(1)}, u32[]{:S(2)}, u32[]{:S(2)}) async-start(f32[32,9,128]{2,1,0:T(8,128)} %pad_maximum_fusion.1), calls=%async_computation | async-start | bytes 524288 | tf_op jit(solution)/shard_map/all_to_all | solution.py:222
  11.6 1.4 copy-start
  55.3 1.7 %copy-start.2 = (f32[512,128]{1,0:T(8,128)S(1)}, f32[512,128]{1,0:T(8,128)}, u32[]{:S(2)}) copy-start(f32[512,128]{1,0:T(8,128)} %depth_ref.1) | copy-start | bytes 786436
  55.3 1.7 %copy-start.3 = (f32[512,128]{1,0:T(8,128)S(1)}, f32[512,128]{1,0:T(8,128)}, u32[]{:S(2)}) copy-start(f32[512,128]{1,0:T(8,128)} %mobility_ref.1) | copy-start | bytes 786436
  55.3 1.7 %copy-start.4 = (f32[2,128,128]{2,1,0:T(8,128)S(1)}, f32[2,128,128]{2,1,0:T(8,128)}, u32[]{:S(2)}) copy-start(f32[2,128,128]{2,1,0:T(8,128)} %precision_ref.1) | copy-start | bytes 393220
  55.3 1.7 %copy-start.5 = (f32[6]{0:T(128)S(1)}, f32[6]{0:T(128)}, u32[]{:S(2)}) copy-start(f32[6]{0:T(128)} %scale_ref.1) | copy-start | bytes 76
  116.4 40.8 %copy-start.1 = (f32[6,512,128]{2,1,0:T(8,128)S(1)}, f32[6,512,128]{2,1,0:T(8,128)}, u32[]{:S(2)}) copy-start(f32[6,512,128]{2,1,0:T(8,128)} %x_ref.1) | copy-start | bytes 4718596

commit v2 on v1

--- a/solution.py
+++ b/solution.py
@@ -249,6 +249,7 @@
     around = neighbours(("gx", "gy"), counts)
     greet(around)
     base = CHUNK
+    part_rows = (rows + CHUNK) // 2
     row_low, col_low = lax.axis_index("gy") * rows, lax.axis_index("gx") * cols
 
     def start(row):
@@ -340,42 +341,49 @@
 
     def sweep(body):
         def one(i, carry):
-            row = CHUNK // 2 + i * CHUNK
-            row_id = lax.broadcasted_iota(jnp.int32, (CHUNK, width), 0) + (row - base + row_low)
-            lane = lax.broadcasted_iota(jnp.int32, (CHUNK, width), 1)
-            col_id = jnp.where(lane < cols + cols // 2, lane, lane - width) + col_low
-            inside = (
-                (row_id >= 0)
-                & (row_id < rows * counts[1])
-                & (col_id >= 0)
-                & (col_id < cols * counts[0])
-            )
+            row = CHUNK // 2 + i * part_rows
+            part = pl.ds(pl.multiple_of(row, 8), part_rows)
+            inside = st[10, part, :]
 
             def mid(p):
-                return st[p, start(row), :]
+                return st[p, part, :]
 
             def tall(p):
-                return st[p, pl.ds(pl.multiple_of(row - 8, 8), CHUNK + 16), :]
+                return st[p, pl.ds(pl.multiple_of(row - 8, 8), part_rows + 16), :]
 
             def put(p, value):
-                st[p, start(row), :] = jnp.where(inside, value, 0.0)
+                st[p, part, :] = value * inside
 
             body(mid, tall, put)
             return carry
 
-        lax.fori_loop(0, (rows + CHUNK) // CHUNK, one, 0)
+        lax.fori_loop(0, 2, one, 0)
+
+    def mask(i, carry):
+        row = CHUNK // 2 + i * CHUNK
+        row_id = lax.broadcasted_iota(jnp.int32, (CHUNK, width), 0) + (row - base + row_low)
+        lane = lax.broadcasted_iota(jnp.int32, (CHUNK, width), 1)
+        col_id = jnp.where(lane < cols + cols // 2, lane, lane - width) + col_low
+        inside = (
+            (row_id >= 0)
+            & (row_id < rows * counts[1])
+            & (col_id >= 0)
+            & (col_id < cols * counts[0])
+        )
+        st[10, start(row), :] = jnp.where(inside, 1.0, 0.0)
+        return carry
 
     def dx(value):
         return 0.5 * (pltpu.roll(value, width - 1, 1) - pltpu.roll(value, 1, 1))
 
     def dy(window):
-        return 0.5 * (window[9 : 9 + CHUNK] - window[7 : 7 + CHUNK])
+        return 0.5 * (window[9 : 9 + part_rows] - window[7 : 7 + part_rows])
 
     def lap(window):
-        value = window[8 : 8 + CHUNK]
+        value = window[8 : 8 + part_rows]
         return (
-            window[9 : 9 + CHUNK]
-            + window[7 : 7 + CHUNK]
+            window[9 : 9 + part_rows]
+            + window[7 : 7 + part_rows]
             + pltpu.roll(value, width - 1, 1)
             + pltpu.roll(value, 1, 1)
             - 4.0 * value
@@ -383,8 +391,8 @@
 
     def silt(now, j, tall):
         window = tall(now + j)
-        value = window[8 : 8 + CHUNK]
-        return value, (
+        value = window[8 : 8 + part_rows]
+        return (
             value
             + TIME_STEP * DIFFUSION[j] * lap(window)
             - TIME_STEP * SETTLING[j] * value
@@ -397,6 +405,7 @@
         st[p, inner, 0:cols] = scale_ref[field] * x_ref[field]
     st[6, inner, 0:cols] = depth_ref[...]
     st[7, inner, 0:cols] = mobility_ref[...]
+    lax.fori_loop(0, (rows + CHUNK) // CHUNK, mask, 0)
     exchange(0)
 
     keep = 1.0 - TIME_STEP * FRICTION
@@ -406,19 +415,19 @@
 
         def levels(mid, tall, put):
             u, v, depth, mobility = tall(2), tall(3), tall(6), tall(7)
-            part = slice(8, 8 + CHUNK)
+            part = slice(8, 8 + part_rows)
             flow = dx(depth[part] * u[part]) + dy(depth * v)
             load = dx(mobility[part] * u[part]) + dy(mobility * v)
-            one, one_new = silt(now, 0, tall)
-            two, two_new = silt(now, 1, tall)
+            one, two = mid(now), mid(now + 1)
             put(0, mid(0) - TIME_STEP * flow)
             put(1, mid(1) - TIME_STEP * load + TIME_STEP * (SETTLING[0] * one + SETTLING[1] * two))
-            put(later, one_new)
-            put(later + 1, two_new)
+            if step < STEPS - 1:
+                for j in range(2):
+                    put(later + j, silt(now, j, tall))
 
         def speeds(mid, tall, put):
             surface = tall(0) + tall(1)
-            put(2, keep * mid(2) - TIME_STEP * GRAVITY * dx(surface[8 : 8 + CHUNK]))
+            put(2, keep * mid(2) - TIME_STEP * GRAVITY * dx(surface[8 : 8 + part_rows]))
             put(3, keep * mid(3) - TIME_STEP * GRAVITY * dy(surface))
 
         sweep(levels)
@@ -446,12 +455,14 @@
 
         def adj_speeds(mid, tall, put):
             height, bed, depth, mobility = tall(0), tall(1), mid(6), mid(7)
-            part = slice(8, 8 + CHUNK)
-            put(2, keep * mid(2) + TIME_STEP * (depth * dx(height[part]) + mobility * dx(bed[part])))
-            put(3, keep * mid(3) + TIME_STEP * (depth * dy(height) + mobility * dy(bed)))
+            part = slice(8, 8 + part_rows)
+            push_x = TIME_STEP * (depth * dx(height[part]) + mobility * dx(bed[part]))
+            push_y = TIME_STEP * (depth * dy(height) + mobility * dy(bed))
+            put(2, push_x if step == 0 else keep * mid(2) + push_x)
+            put(3, push_y if step == 0 else keep * mid(3) + push_y)
             for j in range(2):
-                _, new = silt(now, j, tall)
-                put(later + j, new + TIME_STEP * SETTLING[j] * bed[part])
+                gain = TIME_STEP * SETTLING[j] * bed[part]
+                put(later + j, gain if step == 0 else silt(now, j, tall) + gain)
 
         if step > 0:
             sweep(adj_levels)
@@ -473,7 +484,7 @@
         in_specs=[full, pl.BlockSpec(memory_space=pltpu.SMEM)] + [full] * 5,
         out_specs=full,
         scratch_shapes=[
-            pltpu.VMEM((10, rows + 2 * CHUNK, 2 * cols), jnp.float32),
+            pltpu.VMEM((11, rows + 2 * CHUNK, 2 * cols), jnp.float32),
             pltpu.VMEM((2, 2, rows, cols), jnp.float32),
             pltpu.VMEM((2, 2, rows, cols), jnp.float32),
             pltpu.VMEM((2, 2, 8, REACH, 2 * cols), jnp.float32),

time: 159 us -> 141 us (0.89)
  Pallas kernels: 142 us -> 125 us
    pallas_call x1, Pallas kernels: 59.3 us -> 41.7 us  [flow(): pl.pallas_call(functools.partial(flow_kernel, counts), out_shape=jax.Shap...]
  transfers between devices with their start and end apart: 1 -> 1, of which waited for: 0 -> 0; matrix products, arithmetic and copies ran while one was open for 1% -> 1% of each run, Pallas kernels for 27% -> 30%
where the time goes in v2:
time: 141 us
  Pallas kernels  125 us (89%)
  starting transfers between devices  6.1 us (4%)
  other arithmetic  4.85 us (3%)
  local copies, waits for them, and re-layouts  3.44 us (2%)
    pallas_call x2, Pallas kernels, correlate(): pl.pallas_call(functools.partial(correlate_kernel, counts), out_shape=jax...  83 us
    pallas_call x1, Pallas kernels, flow(): pl.pallas_call(functools.partial(flow_kernel, counts), out_shape=jax.Shap...  41.7 us
    all_to_all x1, starting transfers between devices, observation_sums(): lax.all_to_all(sent, ('gx', 'gy'), split_axis=0, concat_axis=0, tiled=True)  6.1 us
    unnamed x14, local copies, waits for them, and re-layouts  2.96 us
  transfers between devices with their start and end apart: 1, of which 0 were waited for; matrix products, arithmetic and copies ran while one was open for 1% of the time, Pallas kernels for 30%

profile of v2, /device:TPU:4, one launch (start us, length us, event | category | flops | bytes accessed | tf_op | source)
XLA Modules:
  0.0 140.8 jit_solution(16532844488869781159)
XLA Ops:
  0.0 0.8 copy.14
  0.8 0.7 fusion.12
  1.5 1.6 %pad_maximum_fusion.1 = f32[32,9,128]{2,1,0:T(8,128)} fusion(f32[32,1,128]{2,1,0:T(1,128)S(1)} %bitcast.20, f32[32,8,128]{2,1,0:T(8,128)} %bitcast.19), kind=kLoop, calls=%fused_computation.9 | loop fusion | flops 36864 | bytes 294912 | tf_op jit(solution)/shard_map/concatenate | solution.py:221
  3.1 6.1 %all-to-all-start = ((f32[32,9,128]{2,1,0:T(8,128)}), f32[32,9,128]{2,1,0:T(8,128)S(1)}, u32[]{:S(2)}, u32[]{:S(2)}) async-start(f32[32,9,128]{2,1,0:T(8,128)} %pad_maximum_fusion.1), calls=%async_computation | async-start | bytes 524288 | tf_op jit(solution)/shard_map/all_to_all | solution.py:222
  9.2 0.7 fusion.15
  10.7 0.8 copy.13
  11.4 0.1 eq.41
  11.5 0.1 fusion.11.taps_ref
  11.6 0.0 copy-start
  11.6 1.4 copy-done
  13.0 42.3 %shard_map.91.x_ref = f32[6,512,128]{2,1,0:T(8,128)S(1)} custom-call(f32[6,512,128]{2,1,0:T(8,128)S(1)} %copy-done, f32[384,128]{1,0:T(8,128)S(1)} %fusion.11.taps_ref), custom_call_target="tpu_custom_call" | custom-call | flops 1811939328 | bytes 100663296 | tf_op jit(solution)/shard_map/pallas_call | solution.py:189
  55.3 0.0 copy-start.2
  55.3 0.0 copy-start.3
  55.3 0.0 copy-start.4
  55.3 0.0 copy-start.5
  55.3 0.0 all-to-all-done
  55.4 0.1 compare_reduce_fusion.1
  55.5 0.1 eq.47
  55.6 0.1 eq.50
  55.7 0.3 convert_reduce_fusion.1
  55.9 0.4 convolution_bitcast_fusion.1
  56.3 0.4 convolution_bitcast_fusion
  56.8 0.2 broadcast_in_dim.28.seen_ref
  57.0 0.0 copy-done.2
  57.0 0.0 copy-done.3
  57.0 0.0 copy-done.4
  57.0 0.0 copy-done.5
  57.0 41.7 %shard_map.92.x_ref = f32[6,512,128]{2,1,0:T(8,128)S(1)} custom-call(f32[6,512,128]{2,1,0:T(8,128)S(1)} %shard_map.91.x_ref, f32[6]{0:T(128)S(1)} %copy-done.5, f32[512,128]{1,0:T(8,128)S(1)} %copy-done.2, f32[512,128]{1,0:T(8,128)S(1)} %copy-done.3, f32[2,512,128]{2,1,0:T(8,128)S(1)} %broadcast_in_dim.28.seen_ref, ...), custom_call_target="tpu_custom_call" | custom-call | tf_op jit(solution)/shard_map/pallas_call | solution.py:481
  98.7 0.0 copy-start.1
  98.7 40.8 %shard_map.93 = f32[6,512,128]{2,1,0:T(8,128)S(1)} custom-call(f32[6,512,128]{2,1,0:T(8,128)S(1)} %shard_map.92.x_ref, f32[384,128]{1,0:T(8,128)S(1)} %fusion.11.taps_ref), custom_call_target="tpu_custom_call" | custom-call | flops 1811939328 | bytes 100663296 | tf_op jit(solution)/shard_map/pallas_call | solution.py:189
  139.5 0.0 copy-done.1
  139.5 1.3 add.26
  (3 shorter events, 0.1 us)
Async XLA Ops:
  3.1 52.2 %all-to-all-start = ((f32[32,9,128]{2,1,0:T(8,128)}), f32[32,9,128]{2,1,0:T(8,128)S(1)}, u32[]{:S(2)}, u32[]{:S(2)}) async-start(f32[32,9,128]{2,1,0:T(8,128)} %pad_maximum_fusion.1), calls=%async_computation | async-start | bytes 524288 | tf_op jit(solution)/shard_map/all_to_all | solution.py:222
  11.6 1.4 %copy-start = (f32[6,512,128]{2,1,0:T(8,128)S(1)}, f32[6,512,128]{2,1,0:T(8,128)}, u32[]{:S(2)}) copy-start(f32[6,512,128]{2,1,0:T(8,128)} %x_ref.1) | copy-start | bytes 4718596
  55.3 1.7 %copy-start.2 = (f32[512,128]{1,0:T(8,128)S(1)}, f32[512,128]{1,0:T(8,128)}, u32[]{:S(2)}) copy-start(f32[512,128]{1,0:T(8,128)} %depth_ref.1) | copy-start | bytes 786436
  55.3 1.7 %copy-start.3 = (f32[512,128]{1,0:T(8,128)S(1)}, f32[512,128]{1,0:T(8,128)}, u32[]{:S(2)}) copy-start(f32[512,128]{1,0:T(8,128)} %mobility_ref.1) | copy-start | bytes 786436
  55.3 1.7 %copy-start.4 = (f32[2,128,128]{2,1,0:T(8,128)S(1)}, f32[2,128,128]{2,1,0:T(8,128)}, u32[]{:S(2)}) copy-start(f32[2,128,128]{2,1,0:T(8,128)} %precision_ref.1) | copy-start | bytes 393220
  55.3 1.7 %copy-start.5 = (f32[6]{0:T(128)S(1)}, f32[6]{0:T(128)}, u32[]{:S(2)}) copy-start(f32[6]{0:T(128)} %scale_ref.1) | copy-start | bytes 76
  98.7 40.8 %copy-start.1 = (f32[6,512,128]{2,1,0:T(8,128)S(1)}, f32[6,512,128]{2,1,0:T(8,128)}, u32[]{:S(2)}) copy-start(f32[6,512,128]{2,1,0:T(8,128)} %x_ref.1) | copy-start | bytes 4718596

commit v3 on v2

--- a/solution.py
+++ b/solution.py
@@ -291,39 +291,44 @@
             def _():
                 act(copy(phase, way))
 
+    band = rows // 4
+
+    def piece(row):
+        return pl.ds(pl.multiple_of(row, 8), band)
+
     def exchange(phase):
         planes = 8 if phase == 0 else 2
-        lane = lax.broadcasted_iota(jnp.int32, (CHUNK, cols), 1)
+        lane = lax.broadcasted_iota(jnp.int32, (band, cols), 1)
 
         def fill(i, carry):
-            to_low = jnp.zeros((CHUNK, cols), jnp.float32)
+            to_low = jnp.zeros((band, cols), jnp.float32)
             to_high = to_low
             for p in range(planes):
-                block = st[p, start(base + i * CHUNK), 0:cols]
+                block = st[p, piece(base + i * band), 0:cols]
                 here = (lane >= REACH * p) & (lane < REACH * (p + 1))
                 first = block if p == 0 else pltpu.roll(block, REACH * p, 1)
                 to_low = jnp.where(here, first, to_low)
                 to_high = jnp.where(here, pltpu.roll(block, REACH * p + REACH, 1), to_high)
-            pack[phase, 0, start(i * CHUNK), :] = to_low
-            pack[phase, 1, start(i * CHUNK), :] = to_high
+            pack[phase, 0, piece(i * band), :] = to_low
+            pack[phase, 1, piece(i * band), :] = to_high
             return carry
 
-        lax.fori_loop(0, rows // CHUNK, fill, 0)
+        lax.fori_loop(0, 4, fill, 0)
         each(phase, ((0, 0), (1, 1)), lambda c: c.start())
         each(phase, ((0, 1), (1, 0)), lambda c: c.wait_recv())
 
         def spread(i, carry):
-            from_low = got[phase, 0, start(i * CHUNK), :]
-            from_high = got[phase, 1, start(i * CHUNK), :]
+            from_low = got[phase, 0, piece(i * band), :]
+            from_high = got[phase, 1, piece(i * band), :]
             for p in range(planes):
                 high = from_high if p == 0 else pltpu.roll(from_high, cols - REACH * p, 1)
                 low = pltpu.roll(from_low, cols - REACH - REACH * p, 1)
-                st[p, start(base + i * CHUNK), cols:width] = jnp.where(
+                st[p, piece(base + i * band), cols:width] = jnp.where(
                     lane < REACH, high, jnp.where(lane >= cols - REACH, low, 0.0)
                 )
             return carry
 
-        lax.fori_loop(0, rows // CHUNK, spread, 0)
+        lax.fori_loop(0, 4, spread, 0)
         each(phase, ((2, 2), (3, 3)), lambda c: c.start())
         each(phase, ((2, 3), (3, 2)), lambda c: c.wait_recv())
 

time: 141 us -> 138 us (0.979)
  Pallas kernels: 125 us -> 121 us
    pallas_call x1, Pallas kernels: 41.7 us -> 38.4 us  [flow(): pl.pallas_call(functools.partial(flow_kernel, counts), out_shape=jax.Shap...]
  transfers between devices with their start and end apart: 1 -> 1, of which waited for: 0 -> 0; matrix products, arithmetic and copies ran while one was open for 1% -> 1% of each run, Pallas kernels for 30% -> 31%
where the time goes in v3:
time: 138 us
  Pallas kernels  121 us (88%)
  starting transfers between devices  6.1 us (4%)
  other arithmetic  4.85 us (4%)
  local copies, waits for them, and re-layouts  3.44 us (2%)
    pallas_call x2, Pallas kernels, correlate(): pl.pallas_call(functools.partial(correlate_kernel, counts), out_shape=jax...  83 us
    pallas_call x1, Pallas kernels, flow(): pl.pallas_call(functools.partial(flow_kernel, counts), out_shape=jax.Shap...  38.4 us
    all_to_all x1, starting transfers between devices, observation_sums(): lax.all_to_all(sent, ('gx', 'gy'), split_axis=0, concat_axis=0, tiled=True)  6.1 us
    unnamed x14, local copies, waits for them, and re-layouts  2.96 us
  transfers between devices with their start and end apart: 1, of which 0 were waited for; matrix products, arithmetic and copies ran while one was open for 1% of the time, Pallas kernels for 31%

profile of v3, /device:TPU:4, one launch (start us, length us, event | category | flops | bytes accessed | tf_op | source)
XLA Modules:
  0.0 137.5 jit_solution(8123266293768330964)
XLA Ops:
  0.0 0.8 copy.14
  0.8 0.7 fusion.12
  1.5 1.6 %pad_maximum_fusion.1 = f32[32,9,128]{2,1,0:T(8,128)} fusion(f32[32,1,128]{2,1,0:T(1,128)S(1)} %bitcast.20, f32[32,8,128]{2,1,0:T(8,128)} %bitcast.19), kind=kLoop, calls=%fused_computation.9 | loop fusion | flops 36864 | bytes 294912 | tf_op jit(solution)/shard_map/concatenate | solution.py:221
  3.1 6.1 %all-to-all-start = ((f32[32,9,128]{2,1,0:T(8,128)}), f32[32,9,128]{2,1,0:T(8,128)S(1)}, u32[]{:S(2)}, u32[]{:S(2)}) async-start(f32[32,9,128]{2,1,0:T(8,128)} %pad_maximum_fusion.1), calls=%async_computation | async-start | bytes 524288 | tf_op jit(solution)/shard_map/all_to_all | solution.py:222
  9.2 0.7 fusion.15
  10.7 0.8 copy.13
  11.4 0.1 eq.41
  11.5 0.1 fusion.11.taps_ref
  11.6 0.0 copy-start
  11.6 1.4 %copy-done = f32[6,512,128]{2,1,0:T(8,128)S(1)} copy-done((f32[6,512,128]{2,1,0:T(8,128)S(1)}, f32[6,512,128]{2,1,0:T(8,128)}, u32[]{:S(2)}) %copy-start) | copy-done | bytes 1572888
  13.0 42.3 %shard_map.91.x_ref = f32[6,512,128]{2,1,0:T(8,128)S(1)} custom-call(f32[6,512,128]{2,1,0:T(8,128)S(1)} %copy-done, f32[384,128]{1,0:T(8,128)S(1)} %fusion.11.taps_ref), custom_call_target="tpu_custom_call" | custom-call | flops 1811939328 | bytes 100663296 | tf_op jit(solution)/shard_map/pallas_call | solution.py:189
  55.3 0.0 copy-start.2
  55.3 0.0 copy-start.3
  55.3 0.0 copy-start.4
  55.3 0.0 copy-start.5
  55.3 0.0 all-to-all-done
  55.4 0.1 compare_reduce_fusion.1
  55.5 0.1 eq.47
  55.6 0.1 eq.50
  55.7 0.3 convert_reduce_fusion.1
  55.9 0.4 convolution_bitcast_fusion.1
  56.3 0.4 convolution_bitcast_fusion
  56.8 0.2 broadcast_in_dim.28.seen_ref
  57.0 0.0 copy-done.2
  57.0 0.0 copy-done.3
  57.0 0.0 copy-done.4
  57.0 0.0 copy-done.5
  57.0 38.4 %shard_map.92.x_ref = f32[6,512,128]{2,1,0:T(8,128)S(1)} custom-call(f32[6,512,128]{2,1,0:T(8,128)S(1)} %shard_map.91.x_ref, f32[6]{0:T(128)S(1)} %copy-done.5, f32[512,128]{1,0:T(8,128)S(1)} %copy-done.2, f32[512,128]{1,0:T(8,128)S(1)} %copy-done.3, f32[2,512,128]{2,1,0:T(8,128)S(1)} %broadcast_in_dim.28.seen_ref, ...), custom_call_target="tpu_custom_call" | custom-call | tf_op jit(solution)/shard_map/pallas_call | solution.py:486
  95.4 0.0 copy-start.1
  95.4 40.8 %shard_map.93 = f32[6,512,128]{2,1,0:T(8,128)S(1)} custom-call(f32[6,512,128]{2,1,0:T(8,128)S(1)} %shard_map.92.x_ref, f32[384,128]{1,0:T(8,128)S(1)} %fusion.11.taps_ref), custom_call_target="tpu_custom_call" | custom-call | flops 1811939328 | bytes 100663296 | tf_op jit(solution)/shard_map/pallas_call | solution.py:189
  136.2 0.0 copy-done.1
  136.2 1.3 add.26
  (3 shorter events, 0.1 us)
Async XLA Ops:
  3.1 52.2 %all-to-all-start = ((f32[32,9,128]{2,1,0:T(8,128)}), f32[32,9,128]{2,1,0:T(8,128)S(1)}, u32[]{:S(2)}, u32[]{:S(2)}) async-start(f32[32,9,128]{2,1,0:T(8,128)} %pad_maximum_fusion.1), calls=%async_computation | async-start | bytes 524288 | tf_op jit(solution)/shard_map/all_to_all | solution.py:222
  11.6 1.4 %copy-start = (f32[6,512,128]{2,1,0:T(8,128)S(1)}, f32[6,512,128]{2,1,0:T(8,128)}, u32[]{:S(2)}) copy-start(f32[6,512,128]{2,1,0:T(8,128)} %x_ref.1) | copy-start | bytes 4718596
  55.3 1.7 %copy-start.2 = (f32[512,128]{1,0:T(8,128)S(1)}, f32[512,128]{1,0:T(8,128)}, u32[]{:S(2)}) copy-start(f32[512,128]{1,0:T(8,128)} %depth_ref.1) | copy-start | bytes 786436
  55.3 1.7 %copy-start.3 = (f32[512,128]{1,0:T(8,128)S(1)}, f32[512,128]{1,0:T(8,128)}, u32[]{:S(2)}) copy-start(f32[512,128]{1,0:T(8,128)} %mobility_ref.1) | copy-start | bytes 786436
  55.3 1.7 %copy-start.4 = (f32[2,128,128]{2,1,0:T(8,128)S(1)}, f32[2,128,128]{2,1,0:T(8,128)}, u32[]{:S(2)}) copy-start(f32[2,128,128]{2,1,0:T(8,128)} %precision_ref.1) | copy-start | bytes 393220
  55.3 1.7 %copy-start.5 = (f32[6]{0:T(128)S(1)}, f32[6]{0:T(128)}, u32[]{:S(2)}) copy-start(f32[6]{0:T(128)} %scale_ref.1) | copy-start | bytes 76
  95.4 40.8 %copy-start.1 = (f32[6,512,128]{2,1,0:T(8,128)S(1)}, f32[6,512,128]{2,1,0:T(8,128)}, u32[]{:S(2)}) copy-start(f32[6,512,128]{2,1,0:T(8,128)} %x_ref.1) | copy-start | bytes 4718596
